TPU v7x, 32 devices: a whole 2x2x4 slice. The times are simulated.
32 devices in a mesh: groups: 2 (over x), rows: 8 (over z, y), cols: 2 (over core).
Axes of the slice: x: 2, y: 2, z: 4, core: 2. Of those that a mesh axis runs over, the one named last changes fastest.
Arguments:
- depth: float32 [4096, 512], P(('groups', 'rows'), 'cols'), parts along dimension 0, may hold values from 0 to 1.5, as said below
- velocity: float32 [2, 4096, 512], P(None, ('groups', 'rows'), 'cols'), parts along dimension 1, may hold values from -1 to 1
- bed: float32 [4096, 512], P(('groups', 'rows'), 'cols'), parts along dimension 0, may hold values from 0 to 0.5
- slots: int32 [16, 2, 3], P(('groups', 'rows'), 'cols'), parts along dimension 0, may hold values from -1 to 63, as said below
Outputs:
- packed: float32 [16, 2, 3, 3, 128, 128], P(('groups', 'rows'), 'cols'), parts along dimension 0
There are 2 independent parts, one for each index of `groups`. A program takes and returns all parts, laid end to end along the dimension named above; each array names one. Nothing has to cross between parts.
Inputs may be any that keep to these rules, and one draw needn't show every extreme that they name: Each non-negative entry of slots[r, c] is the id of a tile of device (r, c)'s own block (tile rows r * 2 to r * 2 + 1, tile columns c * 2 to c * 2 + 1) or of the block of its partner, device ((r + 4) mod 8, c). No id is listed twice. Every device's partner lists at least one and at most 2 tiles of that device's block, and some device's partner lists exactly 2; at most 3 entries of one list are ids, and some list has exactly 3. `depth`: depth is zero on every cell of a tile that no slot list names.
All inputs are finite; a program needn't handle non-finite values.
Results may differ from a plain program's by a relative error of at most 0.0003.
Values sent between devices are 32-bit elements; how exact they have to be, the bound alone decides.
A program may use at most 64 MiB of HBM per device.

v0:
```python
import jax
import jax.numpy as jnp
from jax import lax
from jax.sharding import PartitionSpec as P

TILE = 128
RT = 2
CT = 2


GRAVITY = 9.81
TIME_STEP = 0.04
DRY_DEPTH = 0.05
SPEED_FLOOR = 0.5


def passed_along(block, axis, distance):
    devices = range(lax.axis_size(axis))
    route = [((i - distance) % len(devices), i) for i in devices]
    return lax.ppermute(block, axis, route)


def with_halo(cells, sides, width):
    for axis, dim in sides:
        count = lax.axis_size(axis)
        ends = count - 1
        head = lax.slice_in_dim(cells, 0, width, axis=dim)
        tail = lax.slice_in_dim(cells, cells.shape[dim] - width, cells.shape[dim], axis=dim)
        cells = jnp.concatenate(
            [
                lax.ppermute(tail, axis, [(i, (i + 1) % count) for i in range(ends)]),
                cells,
                lax.ppermute(head, axis, [((i + 1) % count, i) for i in range(ends)]),
            ],
            axis=dim,
        )
    return cells


def take_range(values, lower_end, upper_end, direction):
    selector = [slice(None)] * values.ndim
    selector[direction] = slice(lower_end, upper_end)
    return values[tuple(selector)]


def minmod(left_diff, right_diff):
    return (
        0.5
        * (jnp.sign(left_diff) + jnp.sign(right_diff))
        * jnp.minimum(jnp.abs(left_diff), jnp.abs(right_diff))
    )


def face_values(values, direction):
    change = take_range(values, 1, None, direction) - take_range(values, 0, -1, direction)
    slope = minmod(take_range(change, 0, -1, direction), take_range(change, 1, None, direction))
    middle = take_range(values, 1, -1, direction)
    return (middle - 0.5 * slope, middle + 0.5 * slope)


def velocity_from(water, flow):
    return 2.0 * water * flow / (water * water + jnp.maximum(water * water, DRY_DEPTH * DRY_DEPTH))


def flux_sweep(water, normal, across, ground, direction):
    water_low, water_high = face_values(water, direction)
    normal_low, normal_high = face_values(normal, direction)
    across_low, across_high = face_values(across, direction)
    ground_low, ground_high = face_values(ground, direction)

    def left_side(values):
        return take_range(values, 0, -1, direction)

    def right_side(values):
        return take_range(values, 1, None, direction)

    water_left = left_side(water_high)
    water_right = right_side(water_low)
    speed_left = velocity_from(water_left, left_side(normal_high))
    speed_right = velocity_from(water_right, right_side(normal_low))
    drift_left = velocity_from(water_left, left_side(across_high))
    drift_right = velocity_from(water_right, right_side(across_low))
    ground_left = left_side(ground_high)
    ground_right = right_side(ground_low)
    ground_top = jnp.maximum(ground_left, ground_right)
    level_left = jnp.maximum(0.0, water_left + ground_left - ground_top)
    level_right = jnp.maximum(0.0, water_right + ground_right - ground_top)
    wave_left = jnp.sqrt(GRAVITY * level_left)
    wave_right = jnp.sqrt(GRAVITY * level_right)
    lower_speed = jnp.minimum(jnp.minimum(speed_left - wave_left, speed_right - wave_right), 0.0)
    upper_speed = jnp.maximum(jnp.maximum(speed_left + wave_left, speed_right + wave_right), 0.0)
    spread = jnp.maximum(upper_speed - lower_speed, SPEED_FLOOR)

    def riemann_flux(flux_left, flux_right, kept_left, kept_right):
        return (
            upper_speed * flux_left
            - lower_speed * flux_right
            + upper_speed * lower_speed * (kept_right - kept_left)
        ) / spread

    mass_left = level_left * speed_left
    mass_right = level_right * speed_right
    mass_flux = riemann_flux(mass_left, mass_right, level_left, level_right)
    push_flux = riemann_flux(
        mass_left * speed_left + 0.5 * GRAVITY * level_left * level_left,
        mass_right * speed_right + 0.5 * GRAVITY * level_right * level_right,
        mass_left,
        mass_right,
    )
    side_flux = riemann_flux(
        mass_left * drift_left,
        mass_right * drift_right,
        level_left * drift_left,
        level_right * drift_right,
    )

    def lower_face(values):
        return take_range(values, 0, -1, direction)

    def upper_face(values):
        return take_range(values, 1, None, direction)

    cell_low = take_range(water_low, 1, -1, direction)
    cell_high = take_range(water_high, 1, -1, direction)
    ground_cell_low = take_range(ground_low, 1, -1, direction)
    ground_cell_high = take_range(ground_high, 1, -1, direction)
    below_level = lower_face(level_right)
    above_level = upper_face(level_left)
    mass_rate = lower_face(mass_flux) - upper_face(mass_flux)
    push_rate = (
        lower_face(push_flux)
        - upper_face(push_flux)
        + 0.5 * GRAVITY * (cell_low * cell_low - below_level * below_level)
        - 0.5 * GRAVITY * (cell_high * cell_high - above_level * above_level)
        + 0.5 * GRAVITY * (cell_low + cell_high) * (ground_cell_low - ground_cell_high)
    )
    side_rate = lower_face(side_flux) - upper_face(side_flux)
    return (mass_rate, push_rate, side_rate)


def advance(state, statics):
    water = state[..., 0, :, :]
    flow_x = state[..., 1, :, :]
    flow_y = state[..., 2, :, :]
    ground = statics[..., 0, :, :]
    active = statics[..., 1, :, :]

    def rows_inner(values):
        return values[..., 2:-2, :]

    def cols_inner(values):
        return values[..., :, 2:-2]

    def center(values):
        return values[..., 2:-2, 2:-2]

    mass_x, push_x, side_x = flux_sweep(
        rows_inner(water), rows_inner(flow_x), rows_inner(flow_y), rows_inner(ground), -1
    )
    mass_y, push_y, side_y = flux_sweep(
        cols_inner(water), cols_inner(flow_y), cols_inner(flow_x), cols_inner(ground), -2
    )
    new_water = center(water) + TIME_STEP * (mass_x + mass_y)
    new_flow_x = center(flow_x) + TIME_STEP * (push_x + side_y)
    new_flow_y = center(flow_y) + TIME_STEP * (side_x + push_y)
    updated = jnp.stack([new_water, new_flow_x, new_flow_y], axis=-3)
    keeping = center(active)[..., None, :, :] > 0.5
    return jnp.where(keeping, updated, center(state))


def cut_tiles(block, pick_rows, pick_cols, extent):

    def one_tile(row_pick, col_pick):
        return lax.dynamic_slice(
            block,
            (jnp.int32(0), row_pick * TILE, col_pick * TILE),
            (block.shape[0], extent, extent),
        )

    return jax.vmap(one_tile)(pick_rows, pick_cols)


def owned_tiles(tile_ids, row_index, col_index, tile_cols_all):
    tile_row = tile_ids // tile_cols_all
    tile_col = tile_ids % tile_cols_all
    inside = (tile_ids >= 0) & (tile_row // RT == row_index) & (tile_col // CT == col_index)
    local_row = jnp.clip(tile_row - row_index * RT, 0, RT - 1)
    local_col = jnp.clip(tile_col - col_index * CT, 0, CT - 1)
    return (inside, local_row, local_col)


def as_column(flags):
    return flags[:, None, None, None]


def shards(depth, velocity, bed, slots):
    half = lax.axis_size("rows") // 2
    row_index = lax.axis_index("rows")
    col_index = lax.axis_index("cols")
    tile_cols_all = CT * lax.axis_size("cols")
    move_count = RT * CT // 2
    listed = slots[0, 0]
    partner_list = passed_along(listed, "rows", half)
    block_rows = jnp.arange(RT, dtype=jnp.int32)[:, None]
    block_cols = jnp.arange(CT, dtype=jnp.int32)[None, :]
    block_ids = (row_index * RT + block_rows) * tile_cols_all + col_index * CT + block_cols
    both_lists = jnp.concatenate([listed, partner_list])
    active_tiles = jnp.any(block_ids[:, :, None] == both_lists[None, None, :], axis=-1).astype(
        jnp.float32
    )
    active_cells = jnp.broadcast_to(active_tiles[:, None, :, None], (RT, TILE, CT, TILE)).reshape(
        RT * TILE, CT * TILE
    )
    state = jnp.stack([depth, depth * velocity[0], depth * velocity[1]])
    statics = jnp.stack([bed, active_cells])
    mine_own, mine_row, mine_col = owned_tiles(listed, row_index, col_index, tile_cols_all)
    send_own, send_row, send_col = owned_tiles(partner_list, row_index, col_index, tile_cols_all)
    send_rank = jnp.cumsum(send_own.astype(jnp.int32)) - 1
    picks = (
        send_own[None, :] & (send_rank[None, :] == jnp.arange(move_count, dtype=jnp.int32)[:, None])
    ).astype(jnp.int32)
    out_rows = jnp.sum(picks * send_row[None, :], axis=1)
    out_cols = jnp.sum(picks * send_col[None, :], axis=1)
    out_valid = jnp.sum(picks, axis=1) > 0
    from_partner = (listed >= 0) & jnp.logical_not(mine_own)
    recv_slot = jnp.clip(jnp.cumsum(from_partner.astype(jnp.int32)) - 1, 0, move_count - 1)
    whole = with_halo(jnp.concatenate([state, statics]), (("rows", 1), ("cols", 2)), 4)
    middle = advance(whole[:3], whole[3:])
    state = advance(middle, whole[3:, 2:-2, 2:-2])
    outgoing = jnp.where(as_column(out_valid), cut_tiles(state, out_rows, out_cols, TILE), 0.0)
    received = passed_along(outgoing, "rows", half)
    own_part = cut_tiles(state, mine_row, mine_col, TILE)
    packed = jnp.where(
        as_column(mine_own), own_part, jnp.where(as_column(from_partner), received[recv_slot], 0.0)
    )
    return packed[None, None]


def solution(mesh):
    in_specs = (
        P(("groups", "rows"), "cols"),
        P(None, ("groups", "rows"), "cols"),
        P(("groups", "rows"), "cols"),
        P(("groups", "rows"), "cols", None),
    )
    out_specs = P(("groups", "rows"), "cols", None, None, None, None)
    return jax.shard_map(shards, mesh=mesh, in_specs=in_specs, out_specs=out_specs, check_vma=False)
```

profile of v0, /device:TPU:0, one launch (start us, length us, event | category | flops | bytes accessed | tf_op | source)
XLA Modules:
  0.0 73.5 jit_solution(3947134042088422195)
XLA Ops:
  0.0 4.1 %collective-permute-start = (s32[3]{0:T(128)}, s32[3]{0:T(128)S(1)}, u32[]{:S(2)}, u32[]{:S(2)}) collective-permute-start(s32[3]{0:T(128)} %bitcast.129), channel_id=1, source_target_pairs={{8,0},{10,2},{12,4},{14,6},{0,8},{2,10},{4,12},{6,14},{9,1},{11,3}... | collective-permute-start | bytes 44 | tf_op jit(solution)/shard_map/ppermute | solution.py:20
  4.1 0.7 compare_select_fusion.4
  4.8 0.7 not_and_fusion
  5.6 1.0 %bitcast_dynamic-update-slice_fusion.5 = f32[5,256,256]{2,1,0:T(8,128)S(1)} fusion(f32[256,256]{1,0:T(8,128)} %param.4), kind=kLoop, calls=%fused_computation.301 | loop fusion | bytes 524288
  6.6 1.1 %bitcast_dynamic-update-slice_fusion.4 = f32[5,256,256]{2,1,0:T(8,128)S(1)} fusion(f32[5,256,256]{2,1,0:T(8,128)S(1)} %bitcast_dynamic-update-slice_fusion.5, f32[256,256]{1,0:T(8,128)} %param.4, f32[2,256,256]{2,1,0:T(8,128)} %param.5), kind=kLoop, calls=%fused_computation.299 | loop fusion | flops 65536 | bytes 786432
  8.8 3.4 %collective-permute-start.1 = (f32[5,4,256]{2,1,0:T(4,128)S(1)}, f32[5,4,256]{2,1,0:T(4,128)S(1)}, u32[]{:S(2)}, u32[]{:S(2)}) collective-permute-start(f32[5,4,256]{2,1,0:T(4,128)S(1)} %get-tuple-element.123), channel_id=1, source_target_pairs={{0,2},{2,4},{4,6},{6,8},{8,10},{10,12},{12,14},{1,3},{3,5},{5,7},{... | collective-permute-start | bytes 61448 | tf_op jit(solution)/shard_map/ppermute | solution.py:31
  12.2 1.3 %collective-permute-start.2 = (f32[5,4,256]{2,1,0:T(4,128)S(1)}, f32[5,4,256]{2,1,0:T(4,128)S(1)}, u32[]{:S(2)}, u32[]{:S(2)}) collective-permute-start(f32[5,4,256]{2,1,0:T(4,128)S(1)} %get-tuple-element.124), channel_id=1, source_target_pairs={{2,0},{4,2},{6,4},{8,6},{10,8},{12,10},{14,12},{3,1},{5,3},{7,5},{... | collective-permute-start | bytes 61448 | tf_op jit(solution)/shard_map/ppermute | solution.py:33
  13.9 4.0 %collective-permute-done.2 = f32[5,4,256]{2,1,0:T(4,128)S(1)} collective-permute-done((f32[5,4,256]{2,1,0:T(4,128)S(1)}, f32[5,4,256]{2,1,0:T(4,128)S(1)}, u32[]{:S(2)}, u32[]{:S(2)}) %collective-permute-start.2) | collective-permute-done | bytes 20512 | tf_op jit(solution)/shard_map/ppermute | solution.py:33
  18.3 0.3 copy.23
  18.6 1.3 %collective-permute-start.3 = (f32[5,264,4]{1,2,0:T(4,128)S(1)}, f32[5,264,4]{1,2,0:T(4,128)S(1)}, u32[]{:S(2)}, u32[]{:S(2)}) collective-permute-start(f32[5,264,4]{1,2,0:T(4,128)S(1)} %copy.23), channel_id=1, source_target_pairs={{0,1},{2,3},{4,5},{6,7},{8,9},{10,11},{12,13},{14,15},{16,17},{18,... | collective-permute-start | bytes 63368 | tf_op jit(solution)/shard_map/ppermute | solution.py:31
  19.9 0.3 copy.24
  20.2 1.3 %collective-permute-start.4 = (f32[5,264,4]{1,2,0:T(4,128)S(1)}, f32[5,264,4]{1,2,0:T(4,128)S(1)}, u32[]{:S(2)}, u32[]{:S(2)}) collective-permute-start(f32[5,264,4]{1,2,0:T(4,128)S(1)} %copy.24), channel_id=1, source_target_pairs={{1,0},{3,2},{5,4},{7,6},{9,8},{11,10},{13,12},{15,14},{17,16},{19,... | collective-permute-start | bytes 63368 | tf_op jit(solution)/shard_map/ppermute | solution.py:33
  21.7 0.3 copy.25
  21.9 1.4 %collective-permute-done.4 = f32[5,264,4]{1,2,0:T(4,128)S(1)} collective-permute-done((f32[5,264,4]{1,2,0:T(4,128)S(1)}, f32[5,264,4]{1,2,0:T(4,128)S(1)}, u32[]{:S(2)}, u32[]{:S(2)}) %collective-permute-start.4) | collective-permute-done | bytes 21152 | tf_op jit(solution)/shard_map/ppermute | solution.py:33
  23.3 0.3 copy.26
  23.6 0.8 %pad_maximum_fusion = f32[5,264,264]{2,1,0:T(8,128)S(1)} fusion(f32[5,264,4]{2,1,0:T(8,128)S(1)} %copy.26, f32[5,4,256]{2,1,0:T(4,128)S(1)} %collective-permute-done.2, f32[5,256,256]{2,1,0:T(8,128)S(1)} %constant_dynamic-update-slice_fusion, f32[5,4,256]{2,1,0:T(4,128)S(1)} %collective-permute-done.1, f32[5,264,4]{2,1,0:T(8,128)S(1)} %copy.25), kind=kLoop, calls=%fused_computation.5 | loop fusion | flops 1393920 | bytes 2787840 | tf_op jit(solution)/shard_map/concatenate | solution.py:29
  25.4 0.3 slice_subtract_fusion.13
  25.9 0.3 slice_subtract_fusion.7
  26.5 0.4 slice_subtract_fusion.28
  27.1 0.4 slice_subtract_fusion.29
  27.4 0.3 multiply_multiply_fusion.16
  27.8 0.3 multiply_multiply_fusion.8
  28.1 0.3 slice_subtract_fusion.14
  28.4 0.4 slice_subtract_fusion.27
  28.7 0.3 slice_subtract_fusion.12
  29.0 0.4 slice_subtract_fusion.26
  29.4 0.3 multiply_multiply_fusion.13
  29.7 0.3 multiply_multiply_fusion.9
  30.2 1.0 %fusion.61 = (f32[260,261]{1,0:T(8,128)S(1)}, f32[260,261]{1,0:T(8,128)S(1)}, f32[260,261]{1,0:T(8,128)S(1)}, f32[260,261]{1,0:T(8,128)S(1)}, f32[260,261]{1,0:T(8,128)S(1)}) fusion(f32[260,262]{1,0:T(8,128)S(1)} %multiply_multiply_fusion.16, f32[260,262]{1,0:T(8,128)S(1)} %slice.909, f32[260,262]{1,0:T(8,128)S(1)} %get-tuple-element.136, ...), kind=kLoop, calls=%fused_computation.135 | loop fusion | flops 2917980 | bytes 3528720 | tf_op jit(solution)/shard_map/div | solution.py:95
  31.3 1.1 %fusion.5 = (f32[260,261]{1,0:T(8,128)S(1)}, f32[260,261]{1,0:T(8,128)S(1)}) fusion(f32[260,261]{1,0:T(8,128)S(1)} %get-tuple-element.94, f32[260,261]{1,0:T(8,128)S(1)} %get-tuple-element.93, f32[260,261]{1,0:T(8,128)S(1)} %get-tuple-element.92, f32[260,261]{1,0:T(8,128)S(1)} %get-tuple-element.91, f32[260,262]{1,0:T(8,128)S(1)} %multiply_multiply_fusion.8, ...), kind=kLoop, calls=%fused_computation.31 | loop fusion | flops 3732300 | bytes 3257280 | tf_op jit(solution)/shard_map/div | solution.py:95
  32.3 0.9 %fusion.62 = (f32[261,260]{1,0:T(8,128)S(1)}, f32[261,260]{1,0:T(8,128)S(1)}, f32[261,260]{1,0:T(8,128)S(1)}, f32[261,260]{1,0:T(8,128)S(1)}, f32[261,260]{1,0:T(8,128)S(1)}) fusion(f32[262,260]{1,0:T(8,128)S(1)} %multiply_multiply_fusion.13, f32[262,260]{1,0:T(8,128)S(1)} %slice.936, f32[262,260]{1,0:T(8,128)S(1)} %get-tuple-element.138, ...), kind=kLoop, calls=%fused_computation.138 | loop fusion | flops 2917980 | bytes 3528720 | tf_op jit(solution)/shard_map/div | solution.py:95
  33.2 1.1 %add_divide_fusion.1 = (f32[261,260]{1,0:T(8,128)S(1)}, f32[261,260]{1,0:T(8,128)S(1)}) fusion(f32[261,260]{1,0:T(8,128)S(1)} %get-tuple-element.99, f32[261,260]{1,0:T(8,128)S(1)} %get-tuple-element.98, f32[262,260]{1,0:T(8,128)S(1)} %multiply_multiply_fusion.9, f32[262,260]{1,0:T(8,128)S(1)} %slice.966, f32[261,260]{1,0:T(8,128)S(1)} %get-tuple-element.97, ...), kind=kLoop, calls=%fused_computation.130 | loop fusion | flops 3732300 | bytes 3257280 | tf_op jit(solution)/shard_map/div | solution.py:95
  34.3 0.8 %fusion.34 = f32[1,260,260]{2,1,0:T(8,128)S(1)} fusion(f32[261,260]{1,0:T(8,128)S(1)} %get-tuple-element.117, f32[260,262]{1,0:T(8,128)S(1)} %get-tuple-element.134, f32[260,262]{1,0:T(8,128)S(1)} %get-tuple-element.133, f32[260,261]{1,0:T(8,128)S(1)} %get-tuple-element.94, f32[260,261]{1,0:T(8,128)S(1)} %get-tuple-element.93, ...), kind=kLoop, calls=%fused_computation.74 | loop fusion | flops 1352000 | bytes 3244800 | tf_op jit(solution)/shard_map/stack | solution.py:166
  35.1 0.9 %fusion.20 = (f32[1,260,260]{2,1,0:T(8,128)S(1)}, f32[1,260,260]{2,1,0:T(8,128)S(1)}) fusion(f32[262,260]{1,0:T(8,128)S(1)} %get-tuple-element.140, f32[262,260]{1,0:T(8,128)S(1)} %get-tuple-element.139, f32[261,260]{1,0:T(8,128)S(1)} %get-tuple-element.99, f32[261,260]{1,0:T(8,128)S(1)} %get-tuple-element.98, f32[261,260]{1,0:T(8,128)S(1)} %get-tuple-element.118, ...), kind=kLoop, calls=%fused_computation.51 | loop fusion | flops 1690000 | bytes 4867200 | tf_op jit(solution)/shard_map/stack | solution.py:166
  36.1 0.5 slice_select_fusion
  37.6 0.3 slice_bitcast_fusion.13
  38.7 0.4 slice_subtract_fusion.31
  39.1 0.3 multiply_multiply_fusion.22
  39.6 0.4 slice_subtract_fusion.30
  41.1 0.3 multiply_multiply_fusion.18
  41.8 1.0 %fusion.81 = (f32[256,257]{1,0:T(8,128)S(1)}, f32[256,257]{1,0:T(8,128)S(1)}, f32[256,257]{1,0:T(8,128)S(1)}, f32[256,257]{1,0:T(8,128)S(1)}, f32[256,257]{1,0:T(8,128)S(1)}) fusion(f32[256,258]{1,0:T(8,128)S(1)} %multiply_multiply_fusion.22, f32[256,258]{1,0:T(8,128)S(1)} %slice.1009, f32[256,258]{1,0:T(8,128)S(1)} %get-tuple-element.144, ...), kind=kLoop, calls=%fused_computation.191 | loop fusion | flops 2829056 | bytes 3421184 | tf_op jit(solution)/shard_map/div | solution.py:95
  42.8 0.6 fusion.98
  43.6 1.0 %fusion.68 = (f32[256,257]{1,0:T(8,128)S(1)}, f32[256,257]{1,0:T(8,128)S(1)}) fusion(f32[256,257]{1,0:T(8,128)S(1)} %get-tuple-element.84, f32[256,257]{1,0:T(8,128)S(1)} %get-tuple-element.83, f32[256,257]{1,0:T(8,128)S(1)} %get-tuple-element.82, f32[256,257]{1,0:T(8,128)S(1)} %get-tuple-element.81, f32[256,258]{1,0:T(8,128)S(1)} %multiply_multiply_fusion.18, ...), kind=kLoop, calls=%fused_computation.163 | loop fusion | flops 3618560 | bytes 3158016 | tf_op jit(solution)/shard_map/div | solution.py:95
  44.6 0.7 add_divide_fusion.3
  45.3 0.6 fusion.114
  45.9 0.4 fusion.104
  46.2 0.3 slice_select_fusion.1
  46.5 0.7 copy-done.2
  47.2 4.1 %while.5 = (s32[]{:T(128)}, f32[3,256,256]{2,1,0:T(8,128)S(1)}, s32[2,3]{1,0:T(2,128)S(1)}, f32[2,3,128,128]{3,2,1,0:T(8,128)S(1)}) while((s32[]{:T(128)}, f32[3,256,256]{2,1,0:T(8,128)S(1)}, s32[2,3]{1,0:T(2,128)S(1)}, f32[2,3,128,128]{3,2,1,0:T(8,128)S(1)}) %tuple.108), condition=%wide.while_cond.1.clone, body=%wide.while_body.1.sunk.clone | while | flops 2 | bytes 393325 | solution.py:174
  47.2 0.6 fusion.147
  47.9 1.4 %bitcast_dynamic-update-slice_fusion.11 = f32[2,3,128,128]{3,2,1,0:T(8,128)S(1)} fusion(f32[2,3,128,128]{3,2,1,0:T(8,128)S(1)} %get-tuple-element.244, s32[]{:T(128)} %get-tuple-element.241, f32[3,256,256]{2,1,0:T(8,128)S(1)} %get-tuple-element.246, s32[]{:T(128)} %bitcast.127, s32[]{:T(128)} %bitcast.128), kind=kLoop, calls=%fused_computation.3.clone.1.clone | loop fusion | bytes 393228 | tf_op jit(solution)/shard_map/vmap()/gather
  49.3 0.6 fusion.147
  49.9 1.4 %bitcast_dynamic-update-slice_fusion.11 = f32[2,3,128,128]{3,2,1,0:T(8,128)S(1)} fusion(f32[2,3,128,128]{3,2,1,0:T(8,128)S(1)} %get-tuple-element.244, s32[]{:T(128)} %get-tuple-element.241, f32[3,256,256]{2,1,0:T(8,128)S(1)} %get-tuple-element.246, s32[]{:T(128)} %bitcast.127, s32[]{:T(128)} %bitcast.128), kind=kLoop, calls=%fused_computation.3.clone.1.clone | loop fusion | bytes 393228 | tf_op jit(solution)/shard_map/vmap()/gather
  51.4 0.7 collective-permute-start.5
  52.1 6.5 %while.4 = (s32[]{:T(128)}, f32[3,256,256]{2,1,0:T(8,128)S(1)}, s32[3,3]{1,0:T(4,128)S(1)}, f32[3,3,128,128]{3,2,1,0:T(8,128)S(1)}) while((s32[]{:T(128)}, f32[3,256,256]{2,1,0:T(8,128)S(1)}, s32[3,3]{1,0:T(4,128)S(1)}, f32[3,3,128,128]{3,2,1,0:T(8,128)S(1)}) %tuple.107), condition=%wide.while_cond.clone, body=%wide.while_body.sunk.clone | while | flops 2 | bytes 393325 | solution.py:174
  52.1 0.7 fusion.146
  52.8 1.5 %bitcast_dynamic-update-slice_fusion.10 = f32[3,3,128,128]{3,2,1,0:T(8,128)S(1)} fusion(f32[3,3,128,128]{3,2,1,0:T(8,128)S(1)} %get-tuple-element.256, s32[]{:T(128)} %get-tuple-element.253, f32[3,256,256]{2,1,0:T(8,128)S(1)} %get-tuple-element.258, s32[]{:T(128)} %bitcast.124, s32[]{:T(128)} %bitcast.125), kind=kLoop, calls=%fused_computation.1.clone.1.clone | loop fusion | bytes 393228 | tf_op jit(solution)/shard_map/vmap()/gather
  54.3 0.7 fusion.146
  54.9 1.5 %bitcast_dynamic-update-slice_fusion.10 = f32[3,3,128,128]{3,2,1,0:T(8,128)S(1)} fusion(f32[3,3,128,128]{3,2,1,0:T(8,128)S(1)} %get-tuple-element.256, s32[]{:T(128)} %get-tuple-element.253, f32[3,256,256]{2,1,0:T(8,128)S(1)} %get-tuple-element.258, s32[]{:T(128)} %bitcast.124, s32[]{:T(128)} %bitcast.125), kind=kLoop, calls=%fused_computation.1.clone.1.clone | loop fusion | bytes 393228 | tf_op jit(solution)/shard_map/vmap()/gather
  56.4 0.7 fusion.146
  57.1 1.5 %bitcast_dynamic-update-slice_fusion.10 = f32[3,3,128,128]{3,2,1,0:T(8,128)S(1)} fusion(f32[3,3,128,128]{3,2,1,0:T(8,128)S(1)} %get-tuple-element.256, s32[]{:T(128)} %get-tuple-element.253, f32[3,256,256]{2,1,0:T(8,128)S(1)} %get-tuple-element.258, s32[]{:T(128)} %bitcast.124, s32[]{:T(128)} %bitcast.125), kind=kLoop, calls=%fused_computation.1.clone.1.clone | loop fusion | bytes 393228 | tf_op jit(solution)/shard_map/vmap()/gather
  58.6 13.4 %collective-permute-done.5 = f32[2,3,128,128]{3,2,1,0:T(8,128)S(1)} collective-permute-done((f32[2,3,128,128]{3,2,1,0:T(8,128)S(1)}, f32[2,3,128,128]{3,2,1,0:T(8,128)S(1)}, u32[]{:S(2)}, u32[]{:S(2)}) %collective-permute-start.5) | collective-permute-done | bytes 393248 | tf_op jit(solution)/shard_map/ppermute | solution.py:20
  72.0 0.6 gather_fusion
  72.6 1.0 %fusion = f32[1,1,3,3,128,128]{5,4,3,2,1,0:T(8,128)} fusion(f32[3,3,128,128]{3,2,1,0:T(8,128)S(1)} %gather_fusion, f32[3,3,128,128]{3,2,1,0:T(8,128)S(1)} %get-tuple-element.12, pred[3]{0:T(512)(128)(4,1)S(1)} %get-tuple-element.72, pred[3]{0:T(512)(128)(4,1)S(1)} %get-tuple-element.73), kind=kLoop, calls=%fused_computation.22 | loop fusion | flops 294912 | bytes 1769478 | tf_op jit(solution)/shard_map/jit(_where)/select_n | solution.py:233
  (82 shorter events, 7.6 us)
Async XLA Ops:
  0.0 7.7 %copy-start.4 = (s32[1,1,3]{2,1,0:T(1,128)S(1)}, s32[1,1,3]{2,1,0:T(1,128)}, u32[]{:S(2)}) copy-start(s32[1,1,3]{2,1,0:T(1,128)} %param.7) | copy-start | bytes 40
  0.0 7.6 %copy-start = (f32[256,256]{1,0:T(8,128)S(1)}, f32[256,256]{1,0:T(8,128)}, u32[]{:S(2)}) copy-start(f32[256,256]{1,0:T(8,128)} %param.4) | copy-start | bytes 786436
  0.0 7.6 %copy-start.1 = (f32[2,256,256]{2,1,0:T(8,128)S(1)}, f32[2,256,256]{2,1,0:T(8,128)}, u32[]{:S(2)}) copy-start(f32[2,256,256]{2,1,0:T(8,128)} %param.5) | copy-start | bytes 1572868
  0.0 8.0 %copy-start.3 = (f32[256,256]{1,0:T(8,128)S(1)}, f32[256,256]{1,0:T(8,128)}, u32[]{:S(2)}) copy-start(f32[256,256]{1,0:T(8,128)} %param.6) | copy-start | bytes 786436
  0.0 8.1 %collective-permute-start = (s32[3]{0:T(128)}, s32[3]{0:T(128)S(1)}, u32[]{:S(2)}, u32[]{:S(2)}) collective-permute-start(s32[3]{0:T(128)} %bitcast.129), channel_id=1, source_target_pairs={{8,0},{10,2},{12,4},{14,6},{0,8},{2,10},{4,12},{6,14},{9,1},{11,3}... | collective-permute-start | bytes 44 | tf_op jit(solution)/shard_map/ppermute | solution.py:20
  8.8 5.1 %collective-permute-start.1 = (f32[5,4,256]{2,1,0:T(4,128)S(1)}, f32[5,4,256]{2,1,0:T(4,128)S(1)}, u32[]{:S(2)}, u32[]{:S(2)}) collective-permute-start(f32[5,4,256]{2,1,0:T(4,128)S(1)} %get-tuple-element.123), channel_id=1, source_target_pairs={{0,2},{2,4},{4,6},{6,8},{8,10},{10,12},{12,14},{1,3},{3,5},{5,7},{... | collective-permute-start | bytes 61448 | tf_op jit(solution)/shard_map/ppermute | solution.py:31
  12.2 5.7 %collective-permute-start.2 = (f32[5,4,256]{2,1,0:T(4,128)S(1)}, f32[5,4,256]{2,1,0:T(4,128)S(1)}, u32[]{:S(2)}, u32[]{:S(2)}) collective-permute-start(f32[5,4,256]{2,1,0:T(4,128)S(1)} %get-tuple-element.124), channel_id=1, source_target_pairs={{2,0},{4,2},{6,4},{8,6},{10,8},{12,10},{14,12},{3,1},{5,3},{7,5},{... | collective-permute-start | bytes 61448 | tf_op jit(solution)/shard_map/ppermute | solution.py:33
  18.6 3.1 %collective-permute-start.3 = (f32[5,264,4]{1,2,0:T(4,128)S(1)}, f32[5,264,4]{1,2,0:T(4,128)S(1)}, u32[]{:S(2)}, u32[]{:S(2)}) collective-permute-start(f32[5,264,4]{1,2,0:T(4,128)S(1)} %copy.23), channel_id=1, source_target_pairs={{0,1},{2,3},{4,5},{6,7},{8,9},{10,11},{12,13},{14,15},{16,17},{18,... | collective-permute-start | bytes 63368 | tf_op jit(solution)/shard_map/ppermute | solution.py:31
  20.2 3.1 %collective-permute-start.4 = (f32[5,264,4]{1,2,0:T(4,128)S(1)}, f32[5,264,4]{1,2,0:T(4,128)S(1)}, u32[]{:S(2)}, u32[]{:S(2)}) collective-permute-start(f32[5,264,4]{1,2,0:T(4,128)S(1)} %copy.24), channel_id=1, source_target_pairs={{1,0},{3,2},{5,4},{7,6},{9,8},{11,10},{13,12},{15,14},{17,16},{19,... | collective-permute-start | bytes 63368 | tf_op jit(solution)/shard_map/ppermute | solution.py:33
  46.2 1.0 %copy-start.2 = (f32[2,3,128,128]{3,2,1,0:T(8,128)S(1)}, f32[2,3,128,128]{3,2,1,0:T(8,128)}, u32[]{:S(2)}) copy-start(f32[2,3,128,128]{3,2,1,0:T(8,128)} %custom-call.5) | copy-start | bytes 1179652
  51.4 20.6 %collective-permute-start.5 = (f32[2,3,128,128]{3,2,1,0:T(8,128)S(1)}, f32[2,3,128,128]{3,2,1,0:T(8,128)S(1)}, u32[]{:S(2)}, u32[]{:S(2)}) collective-permute-start(f32[2,3,128,128]{3,2,1,0:T(8,128)S(1)} %broadcast_select_fusion), channel_id=1, source_target_pairs={{8,0},{10,2},{12,4},{14,6},{0,8},{2,10},{4,12},{6,14},{9,1},{11,3}... | collective-permute-start | bytes 1179656 | tf_op jit(solution)/shard_map/ppermute | solution.py:20
where the time goes:
time: 73.9 us; the launch traced here: 73.5 us
  other arithmetic  25.1 us (34%)
  waiting for transfers between devices  18.8 us (25%)
  local copies, waits for them, and re-layouts  16.8 us (23%)
  starting transfers between devices  12.1 us (16%)
    ppermute x2, waiting for transfers between devices, passed_along(): return lax.ppermute(block, axis, route)  13.4 us
    gather x15, local copies, waits for them, and re-layouts  10.4 us
    div x8, other arithmetic, riemann_flux(): (upper_speed * flux_left - lower_speed * flux_right + upper_speed * lower...  7.36 us
    ppermute x2, waiting for transfers between devices, with_halo(): lax.ppermute(head, axis, [((i + 1) % count, i) for i in range(ends)])  5.36 us
    ppermute x2, starting transfers between devices, passed_along(): return lax.ppermute(block, axis, route)  4.8 us
    ppermute x2, starting transfers between devices, with_halo(): lax.ppermute(tail, axis, [(i, (i + 1) % count) for i in range(ends)])  4.73 us
    sub x16, other arithmetic, face_values(): take_range(values, 1, None, direction)  3.29 us
    another operation x5, other arithmetic, advance(): updated = jnp.stack([new_water, new_flow_x, new_flow_y], axis=-3)  2.9 us
  transfers between devices with their start and end apart: 6, of which 3 were waited for; matrix products, arithmetic and copies ran while one was open for 15% of the time, Pallas kernels for 0%

commit v1 on v0

v1 whole, which is shorter than its diff:
```python
import functools

import jax
import jax.numpy as jnp
from jax import lax
from jax.experimental import pallas as pl
from jax.experimental.pallas import tpu as pltpu
from jax.sharding import PartitionSpec as P

TILE = 128
RT = 2
CT = 2

GRAVITY = 9.81
TIME_STEP = 0.04
DRY_DEPTH = 0.05
SPEED_FLOOR = 0.5
BANDS = 18
ROWS = 8 * BANDS
MESH = pl.DeviceIdType.MESH


def minmod(a, b):
    return jnp.maximum(jnp.minimum(a, b), 0.0) + jnp.minimum(jnp.maximum(a, b), 0.0)


def face_sweep(own, below, slope, slope_below):
    half = [0.5 * s for s in slope]
    low = [v - s for v, s in zip(own, half)]
    high = [v + 0.5 * s for v, s in zip(below, slope_below)]

    def speeds(h, n, t):
        square = h * h
        w = 2.0 * h / (square + jnp.maximum(square, DRY_DEPTH * DRY_DEPTH))
        return w * n, w * t

    hl, nl, tl, zl = high
    hr, nr, tr, zr = low
    ul, vl = speeds(hl, nl, tl)
    ur, vr = speeds(hr, nr, tr)
    top = jnp.maximum(zl, zr)
    el = jnp.maximum(0.0, hl + zl - top)
    er = jnp.maximum(0.0, hr + zr - top)
    cl = jnp.sqrt(GRAVITY * el)
    cr = jnp.sqrt(GRAVITY * er)
    am = jnp.minimum(jnp.minimum(ul - cl, ur - cr), 0.0)
    ap = jnp.maximum(jnp.maximum(ul + cl, ur + cr), 0.0)
    inv = 1.0 / jnp.maximum(ap - am, SPEED_FLOOR)
    bp = ap * inv
    bm = am * inv
    bb = bp * am
    ml = el * ul
    mr = er * ur
    gl = 0.5 * GRAVITY * el * el
    gr = 0.5 * GRAVITY * er * er
    mass = bp * ml - bm * mr + bb * (er - el)
    push = bp * (ml * ul + gl) - bm * (mr * ur + gr) + bb * (mr - ml)
    side = bp * (ml * vl) - bm * (mr * vr) + bb * (er * vr - el * vl)
    cell_high = own[0] + half[0]
    total = hr + cell_high
    bedterm = 0.5 * GRAVITY * (total * (hr - cell_high) - 2.0 * total * half[3])
    return (mass, push + (bedterm - gr), side), (mass, push - gl, side)


def kernel(n, depth, vel, bed, lists, slots, out,
           strips, colpack, corner, rowgot, colgot, cornergot, listgot, ids,
           ext, tiles, work, mid, part, face, res,
           send_sem, recv_sem, id_sem):
    g = lax.axis_index("groups")
    r = lax.axis_index("rows")
    c = lax.axis_index("cols")
    peer = 1 - c
    half = n // 2
    shifts = (0, 1, n - 1, half, half + 1, half - 1)
    opposite = (0, 2, 1, 3, 5, 4)
    tile_cols_all = CT * 2

    def at(k, other):
        return (g, lax.rem(r + shifts[k], n), peer if other else c)

    barrier = pltpu.get_barrier_semaphore()
    for k in range(6):
        for o in range(2):
            if k or o:
                pl.semaphore_signal(barrier, inc=1, device_id=at(k, o), device_id_type=MESH)

    lane8 = lax.broadcasted_iota(jnp.int32, (8, 128), 1)
    fields = (lambda rs, ls: depth[rs, ls], lambda rs, ls: vel[0, rs, ls],
              lambda rs, ls: vel[1, rs, ls], lambda rs, ls: bed[rs, ls])
    left, right, both = pl.ds(0, 128), pl.ds(128, 128), pl.ds(0, 256)
    for f in range(4):
        for e, rs in enumerate((pl.ds(0, 8), pl.ds(248, 8))):
            strips[e, f] = fields[f](rs, both)
            corner[e, f] = jnp.where(c == 0, fields[f](rs, right), fields[f](rs, left))

    @pl.loop(0, 32)
    def _(b):
        rs = pl.ds(pl.multiple_of(8 * b, 8), 8)
        packed = jnp.zeros((8, 128), jnp.float32)
        for f in range(4):
            slab = jnp.where(c == 0, fields[f](rs, right), fields[f](rs, left))
            packed = jnp.where(lane8 // 8 == f, pltpu.roll(slab, 4 + 8 * f, 1), packed)
        colpack[rs, :] = packed

    pl.semaphore_wait(barrier, 11)

    copies = []

    def send(src, dst, k, o):
        i = len(copies)
        copy = pltpu.make_async_remote_copy(
            src_ref=src, dst_ref=dst, send_sem=send_sem.at[i], recv_sem=recv_sem.at[i],
            device_id=at(k, o), device_id_type=MESH)
        copy.start()
        copies.append(copy)

    send(colpack, colgot, 0, 1)
    send(strips.at[1], rowgot.at[0], 1, 0)
    send(strips.at[0], rowgot.at[1], 2, 0)
    send(corner.at[1], cornergot.at[0], 1, 1)
    send(corner.at[0], cornergot.at[1], 2, 1)
    for k in (3, 0, 1, 2, 4, 5):
        for o in range(2):
            if k or o:
                send(lists, listgot.at[2 * opposite[k] + o], k, o)
    listgot[0] = lists[...]

    @pl.loop(0, 32)
    def _(b):
        rs = pl.ds(pl.multiple_of(8 * b, 8), 8)
        rd = pl.ds(pl.multiple_of(8 * b + 8, 8), 8)
        for j, ls in enumerate((left, right)):
            d = depth[rs, ls]
            ext[0, j, rd, :] = d
            ext[1, j, rd, :] = d * vel[0, rs, ls]
            ext[2, j, rd, :] = d * vel[1, rs, ls]
            ext[3, j, rd, :] = bed[rs, ls]

    for f in range(5):
        work[f, 0:8] = jnp.zeros((8, 256), jnp.float32)
        work[f, ROWS + 8:ROWS + 16] = jnp.zeros((8, 256), jnp.float32)
        if f < 3:
            mid[f, 0:8] = jnp.zeros((8, 256), jnp.float32)
            mid[f, ROWS + 8:ROWS + 16] = jnp.zeros((8, 256), jnp.float32)
            face[f, ROWS + 8:ROWS + 16] = jnp.zeros((8, 256), jnp.float32)

    for copy in copies:
        copy.wait_recv()
    to_ids = pltpu.make_async_copy(listgot, ids, id_sem)
    to_ids.start()

    def put(j, rd, d, a, b, z, keep):
        d = jnp.where(keep, d, 0.0)
        ext[0, j, rd, :] = d
        ext[1, j, rd, :] = d * a
        ext[2, j, rd, :] = d * b
        ext[3, j, rd, :] = jnp.where(keep, z, 0.0)

    for e, (rd, keep) in enumerate(((pl.ds(0, 8), r > 0), (pl.ds(264, 8), r < n - 1))):
        for j, ls in enumerate((left, right)):
            put(j, rd, *(rowgot[e, f, :, ls] for f in range(4)), keep)
        put(2, rd, *(cornergot[e, f] for f in range(4)), keep)

    @pl.loop(0, 32)
    def _(b):
        rs = pl.ds(pl.multiple_of(8 * b, 8), 8)
        rd = pl.ds(pl.multiple_of(8 * b + 8, 8), 8)
        got = colgot[rs, :]
        put(2, rd, *(pltpu.roll(got, 128 - (4 + 8 * f), 1) for f in range(4)), True)

    to_ids.wait()

    def is_active(a, b):
        row = RT * r - 1 + a
        col = CT * c - 1 + b
        inside = (row >= 0) & (row < RT * n) & (col >= 0) & (col < tile_cols_all)
        ident = row * tile_cols_all + col
        k = {0: 2, 1: 0, 2: 0, 3: 1}[a]
        o = 0 if b in (1, 2) else 1
        partner = {0: 3, 1: 4, 2: 5}[k]
        hit = ids[2 * k + o, 0, 0] == ident
        for q in (k, partner):
            for s in range(3):
                hit = hit | (ids[2 * q + o, 0, s] == ident)
        return jnp.where(hit & inside, 1.0, 0.0)

    active = [[is_active(a, b) for b in range(4)] for a in range(4)]
    lower = lane8 < 64
    at_left = (c == 0)
    for i in range(2):
        for j in range(2):
            t = 2 * i + j

            def row_of(a):
                return jnp.broadcast_to(active[a][j + 1], (8, 128)), jnp.where(
                    lower, active[a][j + 2], active[a][j])

            top, middle, bottom = row_of(i), row_of(i + 1), row_of(i + 2)

            @pl.loop(0, BANDS)
            def _(b):
                rs = pl.ds(pl.multiple_of(8 * b, 8), 8)
                rd = pl.ds(pl.multiple_of(8 * b + 128 * i, 8), 8)
                for f in range(4):
                    tiles[t, f, rs, 0:128] = ext[f, j, rd, :]
                    outer = ext[f, 2, rd, :]
                    inner = ext[f, 1 - j, rd, :]
                    if j == 0:
                        tiles[t, f, rs, 128:256] = jnp.where(
                            lower, inner, jnp.where(at_left, 0.0, outer))
                    else:
                        tiles[t, f, rs, 128:256] = jnp.where(
                            lower, jnp.where(at_left, outer, 0.0), inner)
                for h in range(2):
                    tiles[t, 4, rs, 128 * h:128 * h + 128] = jnp.where(
                        b == 0, top[h], jnp.where(b == BANDS - 1, bottom[h], middle[h]))

    def owned(ident):
        safe = jnp.maximum(ident, 0)
        row = lax.div(safe, tile_cols_all)
        col = lax.rem(safe, tile_cols_all)
        mine = (ident >= 0) & (lax.div(row, RT) == r) & (lax.div(col, CT) == c)
        return mine, lax.rem(row, RT) * CT + lax.rem(col, CT)

    def ranked(entries):
        first = second = count = jnp.int32(0)
        for ident in entries:
            mine, tile = owned(ident)
            first = jnp.where(mine & (count == 0), tile, first)
            second = jnp.where(mine & (count == 1), tile, second)
            count = count + jnp.where(mine, 1, 0)
        return first, second

    sent = ranked([ids[6, 0, s] for s in range(3)])
    kept = ranked([slots[s] for s in range(3)])

    row8 = lax.broadcasted_iota(jnp.int32, (8, 256), 0)

    def from_next(cur, nxt):
        edge = row8[:, :cur.shape[1]] == 7
        return jnp.where(edge, pltpu.roll(nxt, 7, 0), pltpu.roll(cur, 7, 0))

    def step(src, bed_ref):
        refs = [src.at[0], src.at[1], src.at[2], bed_ref]
        order = (0, 2, 1, 3)

        def band(b, carry):
            prev_down, prev_slope = carry
            base = pl.multiple_of(8 * b + 8, 8)
            here = pl.ds(base, 8)
            ahead = pl.ds(pl.multiple_of(8 * b + 16, 8), 8)
            v0 = [ref[here, :] for ref in refs]
            down = [pltpu.roll(v, 1, 0) for v in v0]
            vm = [jnp.where(row8 == 0, p, d) for p, d in zip(prev_down, down)]
            vp = [from_next(v, ref[ahead, :]) for v, ref in zip(v0, refs)]
            slope = [minmod(v - m, p - v) for v, m, p in zip(v0, vm, vp)]
            turned = [pltpu.roll(q, 1, 0) for q in slope]
            slope_below = [jnp.where(row8 == 0, p, d) for p, d in zip(prev_slope, turned)]
            pick = lambda vs: [vs[q] for q in order]
            gain, loss = face_sweep(pick(v0), pick(vm), pick(slope), pick(slope_below))
            for q in range(3):
                face[q, here, :] = TIME_STEP * loss[order[q]]
            left_of = [pltpu.roll(v, 1, 1) for v in v0]
            diff = [x - y for x, y in zip(v0, left_of)]
            across = [minmod(d, pltpu.roll(d, 255, 1)) for d in diff]
            across_left = [pltpu.roll(q, 1, 1) for q in across]
            xgain, xloss = face_sweep(v0, left_of, across, across_left)
            for q in range(3):
                part[q, here, :] = v0[q] + TIME_STEP * (
                    xgain[q] + gain[order[q]] - pltpu.roll(xloss[q], 255, 1))
            return down, turned

        zeros = [jnp.zeros((8, 256), jnp.float32)] * 4
        lax.fori_loop(0, BANDS, band, (zeros, zeros))

    def task(k, carry):
        t = jnp.where(k == 0, sent[0], jnp.where(k == 1, sent[1], jnp.where(k == 2, kept[0], kept[1])))

        @pl.loop(0, BANDS)
        def _(b):
            rs = pl.ds(pl.multiple_of(8 * b, 8), 8)
            rd = pl.ds(pl.multiple_of(8 * b + 8, 8), 8)
            for f in range(5):
                work[f, rd, :] = tiles[t, f, rs, :]

        step(work, work.at[3])

        @pl.loop(0, BANDS)
        def _(b):
            rd = pl.ds(pl.multiple_of(8 * b + 8, 8), 8)
            ahead = pl.ds(pl.multiple_of(8 * b + 16, 8), 8)
            keep = work[4, rd, :] > 0.5
            for f in range(3):
                mid[f, rd, :] = jnp.where(
                    keep, part[f, rd, :] - from_next(face[f, rd, :], face[f, ahead, :]), work[f, rd, :])

        step(mid, work.at[3])

        @pl.loop(0, 16)
        def _(b):
            rd = pl.ds(pl.multiple_of(8 * b + 16, 8), 8)
            ahead = pl.ds(pl.multiple_of(8 * b + 24, 8), 8)
            for f in range(3):
                res[k, f, pl.ds(pl.multiple_of(8 * b, 8), 8), :] = (
                    part[f, rd, 0:128] - from_next(face[f, rd, 0:128], face[f, ahead, 0:128]))

        @pl.when(k < 2)
        def _():
            result_copy(k).start()

        return carry

    def result_copy(k):
        return pltpu.make_async_remote_copy(
            src_ref=res.at[k], dst_ref=res.at[4 + k], send_sem=send_sem.at[16 + k],
            recv_sem=recv_sem.at[16 + k], device_id=at(3, 0), device_id_type=MESH)

    lax.fori_loop(0, 4, task, 0)
    for k in range(2):
        result_copy(k).wait_recv()

    own_rank = far_rank = jnp.int32(0)
    for s in range(3):
        ident = slots[s]
        mine, _ = owned(ident)
        far = (ident >= 0) & jnp.logical_not(mine)
        index = jnp.where(mine, 2 + own_rank, jnp.where(far, 4 + far_rank, 2))
        index = jnp.minimum(index, 5)
        own_rank = own_rank + jnp.where(mine, 1, 0)
        far_rank = far_rank + jnp.where(far, 1, 0)

        @pl.loop(0, 16)
        def _(b):
            rs = pl.ds(pl.multiple_of(8 * b, 8), 8)
            for f in range(3):
                out[0, 0, s, f, rs, :] = jnp.where(ident >= 0, res[index, f, rs, :], 0.0)

    for copy in copies:
        copy.wait_send()
    for k in range(2):
        result_copy(k).wait_send()


def shards(depth, velocity, bed, slots):
    n = lax.axis_size("rows")
    listed = slots[0, 0]
    lists = jnp.pad(listed[None, :], ((0, 0), (0, 125)), constant_values=-1)
    vmem = pl.BlockSpec(memory_space=pltpu.VMEM)
    f32 = jnp.float32
    return pl.pallas_call(
        functools.partial(kernel, n),
        out_shape=jax.ShapeDtypeStruct((1, 1, 3, 3, TILE, TILE), f32),
        in_specs=[vmem] * 4 + [pl.BlockSpec(memory_space=pltpu.SMEM)],
        out_specs=vmem,
        scratch_shapes=[
            pltpu.VMEM((2, 4, 8, 256), f32),
            pltpu.VMEM((256, 128), f32),
            pltpu.VMEM((2, 4, 8, 128), f32),
            pltpu.VMEM((2, 4, 8, 256), f32),
            pltpu.VMEM((256, 128), f32),
            pltpu.VMEM((2, 4, 8, 128), f32),
            pltpu.VMEM((12, 1, 128), jnp.int32),
            pltpu.SMEM((12, 1, 128), jnp.int32),
            pltpu.VMEM((4, 3, 272, 128), f32),
            pltpu.VMEM((4, 5, ROWS, 256), f32),
            pltpu.VMEM((5, ROWS + 16, 256), f32),
            pltpu.VMEM((3, ROWS + 16, 256), f32),
            pltpu.VMEM((3, ROWS + 16, 256), f32),
            pltpu.VMEM((3, ROWS + 16, 256), f32),
            pltpu.VMEM((6, 3, TILE, TILE), f32),
            pltpu.SemaphoreType.DMA((18,)),
            pltpu.SemaphoreType.DMA((18,)),
            pltpu.SemaphoreType.DMA,
        ],
        compiler_params=pltpu.CompilerParams(
            collective_id=0, has_side_effects=True, vmem_limit_bytes=40 * 2**20),
    )(depth, velocity, bed, lists, listed)


def solution(mesh):
    in_specs = (
        P(("groups", "rows"), "cols"),
        P(None, ("groups", "rows"), "cols"),
        P(("groups", "rows"), "cols"),
        P(("groups", "rows"), "cols", None),
    )
    out_specs = P(("groups", "rows"), "cols", None, None, None, None)
    return jax.shard_map(shards, mesh=mesh, in_specs=in_specs, out_specs=out_specs, check_vma=False)
```

time: 73.9 us -> 68.4 us (0.926)
  Pallas kernels: 0 us -> 63.8 us
  other arithmetic: 25.1 us -> 0 us
  waiting for transfers between devices: 18.8 us -> 0 us
  local copies, waits for them, and re-layouts: 16.8 us -> 4.42 us
  starting transfers between devices: 12.1 us -> 0 us
    pallas_call x0 -> x1, Pallas kernels: none -> 63.8 us  [shards(): pl.pallas_call(functools.partial(kernel, n), out_shape=jax.ShapeDtypeStru...]
    ppermute x6 -> x0, waiting for transfers between devices: 18.8 us -> none  [the longest x2 13.4 us: passed_along(): return lax.ppermute(block, axis, route)]
    ppermute x6 -> x0, starting transfers between devices: 12.1 us -> none  [the longest x2 4.8 us: passed_along(): return lax.ppermute(block, axis, route)]
    gather x16 -> x0, local copies, waits for them, and re-layouts: 11 us -> none
    div x8 -> x0, other arithmetic: 7.36 us -> none  [riemann_flux(): (upper_speed * flux_left - lower_speed * flux_right + upper_speed * lower...]
    sub x25 -> x0, other arithmetic: 6.04 us -> none  [the longest x16 3.29 us: face_values(): take_range(values, 1, None, direction)]
    another operation x8 -> x0, other arithmetic: 3.28 us -> none  [the longest x5 2.9 us: advance(): updated = jnp.stack([new_water, new_flow_x, new_flow_y], axis=-3)]
    unnamed x14 -> x9, local copies, waits for them, and re-layouts: 1.88 us -> 4.41 us
  transfers between devices with their start and end apart: 6 -> 0, of which waited for: 3 -> 0; matrix products, arithmetic and copies ran while one was open for 15% -> 0% of each run, Pallas kernels for 0% -> 0%
where the time goes in v1:
time: 68.4 us; the launch traced here: 68.2 us
  Pallas kernels  63.8 us (93%)
  local copies, waits for them, and re-layouts  4.42 us (6%)
    pallas_call x1, Pallas kernels, shards(): pl.pallas_call(functools.partial(kernel, n), out_shape=jax.ShapeDtypeStru...  63.8 us
    unnamed x9, local copies, waits for them, and re-layouts  4.41 us

profile of v1, /device:TPU:0, one launch (start us, length us, event | category | flops | bytes accessed | tf_op | source)
XLA Modules:
  0.0 68.2 jit_solution(4011528599853007729)
XLA Ops:
  0.0 0.0 copy-start.3
  0.0 0.7 copy-done.3
  0.7 0.0 copy-start
  0.7 1.0 %copy-done = f32[2,256,256]{2,1,0:T(8,128)S(1)} copy-done((f32[2,256,256]{2,1,0:T(8,128)S(1)}, f32[2,256,256]{2,1,0:T(8,128)}, u32[]{:S(2)}) %copy-start) | copy-done | bytes 524312
  1.7 0.0 copy-start.1
  1.7 0.9 %copy-done.1 = f32[256,256]{1,0:T(8,128)S(1)} copy-done((f32[256,256]{1,0:T(8,128)S(1)}, f32[256,256]{1,0:T(8,128)}, u32[]{:S(2)}) %copy-start.1) | copy-done | bytes 262168
  2.7 0.0 copy-start.2
  2.7 0.9 %copy-done.2 = f32[256,256]{1,0:T(8,128)S(1)} copy-done((f32[256,256]{1,0:T(8,128)S(1)}, f32[256,256]{1,0:T(8,128)}, u32[]{:S(2)}) %copy-start.2) | copy-done | bytes 262168
  3.6 63.8 %shard_map.46 = f32[1,1,3,3,128,128]{5,4,3,2,1,0:T(8,128)S(1)} custom-call(f32[256,256]{1,0:T(8,128)S(1)} %copy-done.1, f32[2,256,256]{2,1,0:T(8,128)S(1)} %copy-done, f32[256,256]{1,0:T(8,128)S(1)} %copy-done.2, s32[1,128]{1,0:T(1,128)S(1)} %pad.4.lists, s32[3]{0:T(128)S(1)} %bitcast.3), custom_call_target="tpu_custom_call" | custom-call | tf_op jit(solution)/shard_map/pallas_call | solution.py:350
  67.4 0.8 %copy.6 = f32[1,1,3,3,128,128]{5,4,3,2,1,0:T(8,128)} copy(f32[1,1,3,3,128,128]{5,4,3,2,1,0:T(8,128)S(1)} %shard_map.46) | data formatting | bytes 1179648
  (1 shorter events, 0.0 us)
Async XLA Ops:
  0.0 0.7 copy-start.3
  0.7 1.0 %copy-start = (f32[2,256,256]{2,1,0:T(8,128)S(1)}, f32[2,256,256]{2,1,0:T(8,128)}, u32[]{:S(2)}) copy-start(f32[2,256,256]{2,1,0:T(8,128)} %vel.1) | copy-start | bytes 1572868
  1.7 0.9 %copy-start.1 = (f32[256,256]{1,0:T(8,128)S(1)}, f32[256,256]{1,0:T(8,128)}, u32[]{:S(2)}) copy-start(f32[256,256]{1,0:T(8,128)} %depth.1) | copy-start | bytes 786436
  2.7 0.9 %copy-start.2 = (f32[256,256]{1,0:T(8,128)S(1)}, f32[256,256]{1,0:T(8,128)}, u32[]{:S(2)}) copy-start(f32[256,256]{1,0:T(8,128)} %bed.1) | copy-start | bytes 786436

commit v2 on v1

--- a/solution.py
+++ b/solution.py
@@ -62,7 +62,8 @@
     return (mass, push + (bedterm - gr), side), (mass, push - gl, side)
 
 
-def kernel(n, depth, vel, bed, lists, slots, out,
+def kernel(n, depth_hbm, vel_hbm, bed_hbm, lists, slots, out,
+           depth, vel, bed, in_sem,
            strips, colpack, corner, rowgot, colgot, cornergot, listgot, ids,
            ext, tiles, work, mid, part, face, res,
            send_sem, recv_sem, id_sem):
@@ -78,12 +79,18 @@
     def at(k, other):
         return (g, lax.rem(r + shifts[k], n), peer if other else c)
 
+    loads = [pltpu.make_async_copy(src, dst, in_sem.at[i]) for i, (src, dst) in enumerate(
+        ((depth_hbm, depth), (vel_hbm, vel), (bed_hbm, bed)))]
+    for load in loads:
+        load.start()
     barrier = pltpu.get_barrier_semaphore()
     for k in range(6):
         for o in range(2):
             if k or o:
                 pl.semaphore_signal(barrier, inc=1, device_id=at(k, o), device_id_type=MESH)
 
+    for load in loads:
+        load.wait()
     lane8 = lax.broadcasted_iota(jnp.int32, (8, 128), 1)
     fields = (lambda rs, ls: depth[rs, ls], lambda rs, ls: vel[0, rs, ls],
               lambda rs, ls: vel[1, rs, ls], lambda rs, ls: bed[rs, ls])
@@ -93,7 +100,7 @@
             strips[e, f] = fields[f](rs, both)
             corner[e, f] = jnp.where(c == 0, fields[f](rs, right), fields[f](rs, left))
 
-    @pl.loop(0, 32)
+    @pl.loop(0, 32, unroll=8)
     def _(b):
         rs = pl.ds(pl.multiple_of(8 * b, 8), 8)
         packed = jnp.zeros((8, 128), jnp.float32)
@@ -125,7 +132,7 @@
                 send(lists, listgot.at[2 * opposite[k] + o], k, o)
     listgot[0] = lists[...]
 
-    @pl.loop(0, 32)
+    @pl.loop(0, 32, unroll=8)
     def _(b):
         rs = pl.ds(pl.multiple_of(8 * b, 8), 8)
         rd = pl.ds(pl.multiple_of(8 * b + 8, 8), 8)
@@ -161,7 +168,7 @@
             put(j, rd, *(rowgot[e, f, :, ls] for f in range(4)), keep)
         put(2, rd, *(cornergot[e, f] for f in range(4)), keep)
 
-    @pl.loop(0, 32)
+    @pl.loop(0, 32, unroll=8)
     def _(b):
         rs = pl.ds(pl.multiple_of(8 * b, 8), 8)
         rd = pl.ds(pl.multiple_of(8 * b + 8, 8), 8)
@@ -197,7 +204,7 @@
 
             top, middle, bottom = row_of(i), row_of(i + 1), row_of(i + 2)
 
-            @pl.loop(0, BANDS)
+            @pl.loop(0, BANDS, unroll=6)
             def _(b):
                 rs = pl.ds(pl.multiple_of(8 * b, 8), 8)
                 rd = pl.ds(pl.multiple_of(8 * b + 128 * i, 8), 8)
@@ -271,12 +278,12 @@
             return down, turned
 
         zeros = [jnp.zeros((8, 256), jnp.float32)] * 4
-        lax.fori_loop(0, BANDS, band, (zeros, zeros))
+        lax.fori_loop(0, BANDS, band, (zeros, zeros), unroll=6)
 
     def task(k, carry):
         t = jnp.where(k == 0, sent[0], jnp.where(k == 1, sent[1], jnp.where(k == 2, kept[0], kept[1])))
 
-        @pl.loop(0, BANDS)
+        @pl.loop(0, BANDS, unroll=6)
         def _(b):
             rs = pl.ds(pl.multiple_of(8 * b, 8), 8)
             rd = pl.ds(pl.multiple_of(8 * b + 8, 8), 8)
@@ -285,7 +292,7 @@
 
         step(work, work.at[3])
 
-        @pl.loop(0, BANDS)
+        @pl.loop(0, BANDS, unroll=6)
         def _(b):
             rd = pl.ds(pl.multiple_of(8 * b + 8, 8), 8)
             ahead = pl.ds(pl.multiple_of(8 * b + 16, 8), 8)
@@ -296,7 +303,7 @@
 
         step(mid, work.at[3])
 
-        @pl.loop(0, 16)
+        @pl.loop(0, 16, unroll=8)
         def _(b):
             rd = pl.ds(pl.multiple_of(8 * b + 16, 8), 8)
             ahead = pl.ds(pl.multiple_of(8 * b + 24, 8), 8)
@@ -329,7 +336,7 @@
         own_rank = own_rank + jnp.where(mine, 1, 0)
         far_rank = far_rank + jnp.where(far, 1, 0)
 
-        @pl.loop(0, 16)
+        @pl.loop(0, 16, unroll=8)
         def _(b):
             rs = pl.ds(pl.multiple_of(8 * b, 8), 8)
             for f in range(3):
@@ -350,9 +357,13 @@
     return pl.pallas_call(
         functools.partial(kernel, n),
         out_shape=jax.ShapeDtypeStruct((1, 1, 3, 3, TILE, TILE), f32),
-        in_specs=[vmem] * 4 + [pl.BlockSpec(memory_space=pltpu.SMEM)],
+        in_specs=[pl.BlockSpec(memory_space=pltpu.HBM)] * 3 + [vmem] + [pl.BlockSpec(memory_space=pltpu.SMEM)],
         out_specs=vmem,
         scratch_shapes=[
+            pltpu.VMEM((256, 256), f32),
+            pltpu.VMEM((2, 256, 256), f32),
+            pltpu.VMEM((256, 256), f32),
+            pltpu.SemaphoreType.DMA((3,)),
             pltpu.VMEM((2, 4, 8, 256), f32),
             pltpu.VMEM((256, 128), f32),
             pltpu.VMEM((2, 4, 8, 128), f32),

time: 68.4 us -> 40.2 us (0.59)
  Pallas kernels: 63.8 us -> 35.5 us
    pallas_call x1, Pallas kernels: 63.8 us -> 35.5 us  [shards(): pl.pallas_call(functools.partial(kernel, n), out_shape=jax.ShapeDtypeStru...]
where the time goes in v2:
time: 40.2 us; the launch traced here: 39.9 us
  Pallas kernels  35.5 us (88%)
  local copies, waits for them, and re-layouts  4.42 us (11%)
    pallas_call x1, Pallas kernels, shards(): pl.pallas_call(functools.partial(kernel, n), out_shape=jax.ShapeDtypeStru...  35.5 us
    unnamed x9, local copies, waits for them, and re-layouts  4.41 us

profile of v2, /device:TPU:0, one launch (start us, length us, event | category | flops | bytes accessed | tf_op | source)
XLA Modules:
  0.0 39.9 jit_solution(5712079347617392398)
XLA Ops:
  0.0 0.0 copy-start.3
  0.0 0.7 %copy-done.3 = s32[1,1,3]{2,1,0:T(1,128)S(1)} copy-done((s32[1,1,3]{2,1,0:T(1,128)S(1)}, s32[1,1,3]{2,1,0:T(1,128)}, u32[]{:S(2)}) %copy-start.3) | copy-done | bytes 36
  0.7 0.0 copy-start
  0.7 1.0 %copy-done = f32[2,256,256]{2,1,0:T(8,128)S(1)} copy-done((f32[2,256,256]{2,1,0:T(8,128)S(1)}, f32[2,256,256]{2,1,0:T(8,128)}, u32[]{:S(2)}) %copy-start) | copy-done | bytes 524312
  1.7 0.0 copy-start.1
  1.7 0.9 %copy-done.1 = f32[256,256]{1,0:T(8,128)S(1)} copy-done((f32[256,256]{1,0:T(8,128)S(1)}, f32[256,256]{1,0:T(8,128)}, u32[]{:S(2)}) %copy-start.1) | copy-done | bytes 262168
  2.7 0.0 copy-start.2
  2.7 0.9 %copy-done.2 = f32[256,256]{1,0:T(8,128)S(1)} copy-done((f32[256,256]{1,0:T(8,128)S(1)}, f32[256,256]{1,0:T(8,128)}, u32[]{:S(2)}) %copy-start.2) | copy-done | bytes 262168
  3.6 35.5 %shard_map.46 = f32[1,1,3,3,128,128]{5,4,3,2,1,0:T(8,128)S(1)} custom-call(f32[256,256]{1,0:T(8,128)S(1)} %copy-done.1, f32[2,256,256]{2,1,0:T(8,128)S(1)} %copy-done, f32[256,256]{1,0:T(8,128)S(1)} %copy-done.2, s32[1,128]{1,0:T(1,128)S(1)} %pad.4.lists, s32[3]{0:T(128)S(1)} %bitcast.3), custom_call_target="tpu_custom_call" | custom-call | tf_op jit(solution)/shard_map/pallas_call | solution.py:357
  39.1 0.8 %copy.6 = f32[1,1,3,3,128,128]{5,4,3,2,1,0:T(8,128)} copy(f32[1,1,3,3,128,128]{5,4,3,2,1,0:T(8,128)S(1)} %shard_map.46) | data formatting | bytes 1179648
  (1 shorter events, 0.0 us)
Async XLA Ops:
  0.0 0.7 %copy-start.3 = (s32[1,1,3]{2,1,0:T(1,128)S(1)}, s32[1,1,3]{2,1,0:T(1,128)}, u32[]{:S(2)}) copy-start(s32[1,1,3]{2,1,0:T(1,128)} %param.7) | copy-start | bytes 40
  0.7 1.0 %copy-start = (f32[2,256,256]{2,1,0:T(8,128)S(1)}, f32[2,256,256]{2,1,0:T(8,128)}, u32[]{:S(2)}) copy-start(f32[2,256,256]{2,1,0:T(8,128)} %vel_hbm.1) | copy-start | bytes 1572868
  1.7 0.9 %copy-start.1 = (f32[256,256]{1,0:T(8,128)S(1)}, f32[256,256]{1,0:T(8,128)}, u32[]{:S(2)}) copy-start(f32[256,256]{1,0:T(8,128)} %depth_hbm.1) | copy-start | bytes 786436
  2.7 0.9 %copy-start.2 = (f32[256,256]{1,0:T(8,128)S(1)}, f32[256,256]{1,0:T(8,128)}, u32[]{:S(2)}) copy-start(f32[256,256]{1,0:T(8,128)} %bed_hbm.1) | copy-start | bytes 786436

commit v3 on v2

--- a/solution.py
+++ b/solution.py
@@ -16,7 +16,10 @@
 DRY_DEPTH = 0.05
 SPEED_FLOOR = 0.5
 BANDS = 18
-ROWS = 8 * BANDS
+PART_ROWS = 64
+PART_BANDS = 10
+ROWS = 8 * PART_BANDS
+VMEM_LIMIT = 63 * 2**20
 MESH = pl.DeviceIdType.MESH
 
 
@@ -62,8 +65,8 @@
     return (mass, push + (bedterm - gr), side), (mass, push - gl, side)
 
 
-def kernel(n, depth_hbm, vel_hbm, bed_hbm, lists, slots, out,
-           depth, vel, bed, in_sem,
+def kernel(n, depth_hbm, vel_hbm, bed_hbm, slots, out,
+           depth, vel, bed, in_sem, lists,
            strips, colpack, corner, rowgot, colgot, cornergot, listgot, ids,
            ext, tiles, work, mid, part, face, res,
            send_sem, recv_sem, id_sem):
@@ -83,6 +86,9 @@
         ((depth_hbm, depth), (vel_hbm, vel), (bed_hbm, bed)))]
     for load in loads:
         load.start()
+    place = lax.broadcasted_iota(jnp.int32, (1, 128), 1)
+    lists[...] = jnp.where(place == 0, slots[0], jnp.where(
+        place == 1, slots[1], jnp.where(place == 2, slots[2], -1)))
     barrier = pltpu.get_barrier_semaphore()
     for k in range(6):
         for o in range(2):
@@ -278,21 +284,23 @@
             return down, turned
 
         zeros = [jnp.zeros((8, 256), jnp.float32)] * 4
-        lax.fori_loop(0, BANDS, band, (zeros, zeros), unroll=6)
-
-    def task(k, carry):
+        lax.fori_loop(0, PART_BANDS, band, (zeros, zeros), unroll=10)
+
+    def task(q, carry):
+        k = lax.div(q, 2)
+        first = PART_ROWS * lax.rem(q, 2)
         t = jnp.where(k == 0, sent[0], jnp.where(k == 1, sent[1], jnp.where(k == 2, kept[0], kept[1])))
 
-        @pl.loop(0, BANDS, unroll=6)
+        @pl.loop(0, PART_BANDS, unroll=5)
         def _(b):
-            rs = pl.ds(pl.multiple_of(8 * b, 8), 8)
+            rs = pl.ds(pl.multiple_of(first + 8 * b, 8), 8)
             rd = pl.ds(pl.multiple_of(8 * b + 8, 8), 8)
             for f in range(5):
                 work[f, rd, :] = tiles[t, f, rs, :]
 
         step(work, work.at[3])
 
-        @pl.loop(0, BANDS, unroll=6)
+        @pl.loop(0, PART_BANDS, unroll=5)
         def _(b):
             rd = pl.ds(pl.multiple_of(8 * b + 8, 8), 8)
             ahead = pl.ds(pl.multiple_of(8 * b + 16, 8), 8)
@@ -303,28 +311,31 @@
 
         step(mid, work.at[3])
 
-        @pl.loop(0, 16, unroll=8)
+        @pl.loop(0, 8, unroll=8)
         def _(b):
             rd = pl.ds(pl.multiple_of(8 * b + 16, 8), 8)
             ahead = pl.ds(pl.multiple_of(8 * b + 24, 8), 8)
             for f in range(3):
-                res[k, f, pl.ds(pl.multiple_of(8 * b, 8), 8), :] = (
+                res[k, f, pl.ds(pl.multiple_of(first + 8 * b, 8), 8), :] = (
                     part[f, rd, 0:128] - from_next(face[f, rd, 0:128], face[f, ahead, 0:128]))
 
-        @pl.when(k < 2)
+        @pl.when(q < 4)
         def _():
-            result_copy(k).start()
+            result_copy(q).start()
 
         return carry
 
-    def result_copy(k):
+    def result_copy(q):
+        k = lax.div(q, 2) if not isinstance(q, int) else q // 2
+        first = pl.multiple_of(PART_ROWS * (lax.rem(q, 2) if not isinstance(q, int) else q % 2), 8)
+        rows = pl.ds(first, PART_ROWS)
         return pltpu.make_async_remote_copy(
-            src_ref=res.at[k], dst_ref=res.at[4 + k], send_sem=send_sem.at[16 + k],
-            recv_sem=recv_sem.at[16 + k], device_id=at(3, 0), device_id_type=MESH)
-
-    lax.fori_loop(0, 4, task, 0)
-    for k in range(2):
-        result_copy(k).wait_recv()
+            src_ref=res.at[k, :, rows, :], dst_ref=res.at[4 + k, :, rows, :], send_sem=send_sem.at[16 + q],
+            recv_sem=recv_sem.at[16 + q], device_id=at(3, 0), device_id_type=MESH)
+
+    lax.fori_loop(0, 8, task, 0)
+    for q in range(4):
+        result_copy(q).wait_recv()
 
     own_rank = far_rank = jnp.int32(0)
     for s in range(3):
@@ -344,26 +355,26 @@
 
     for copy in copies:
         copy.wait_send()
-    for k in range(2):
-        result_copy(k).wait_send()
+    for q in range(4):
+        result_copy(q).wait_send()
 
 
 def shards(depth, velocity, bed, slots):
     n = lax.axis_size("rows")
     listed = slots[0, 0]
-    lists = jnp.pad(listed[None, :], ((0, 0), (0, 125)), constant_values=-1)
     vmem = pl.BlockSpec(memory_space=pltpu.VMEM)
     f32 = jnp.float32
     return pl.pallas_call(
         functools.partial(kernel, n),
         out_shape=jax.ShapeDtypeStruct((1, 1, 3, 3, TILE, TILE), f32),
-        in_specs=[pl.BlockSpec(memory_space=pltpu.HBM)] * 3 + [vmem] + [pl.BlockSpec(memory_space=pltpu.SMEM)],
+        in_specs=[pl.BlockSpec(memory_space=pltpu.HBM)] * 3 + [pl.BlockSpec(memory_space=pltpu.SMEM)],
         out_specs=vmem,
         scratch_shapes=[
             pltpu.VMEM((256, 256), f32),
             pltpu.VMEM((2, 256, 256), f32),
             pltpu.VMEM((256, 256), f32),
             pltpu.SemaphoreType.DMA((3,)),
+            pltpu.VMEM((1, 128), jnp.int32),
             pltpu.VMEM((2, 4, 8, 256), f32),
             pltpu.VMEM((256, 128), f32),
             pltpu.VMEM((2, 4, 8, 128), f32),
@@ -373,19 +384,19 @@
             pltpu.VMEM((12, 1, 128), jnp.int32),
             pltpu.SMEM((12, 1, 128), jnp.int32),
             pltpu.VMEM((4, 3, 272, 128), f32),
-            pltpu.VMEM((4, 5, ROWS, 256), f32),
+            pltpu.VMEM((4, 5, 8 * BANDS, 256), f32),
             pltpu.VMEM((5, ROWS + 16, 256), f32),
             pltpu.VMEM((3, ROWS + 16, 256), f32),
             pltpu.VMEM((3, ROWS + 16, 256), f32),
             pltpu.VMEM((3, ROWS + 16, 256), f32),
             pltpu.VMEM((6, 3, TILE, TILE), f32),
-            pltpu.SemaphoreType.DMA((18,)),
-            pltpu.SemaphoreType.DMA((18,)),
+            pltpu.SemaphoreType.DMA((20,)),
+            pltpu.SemaphoreType.DMA((20,)),
             pltpu.SemaphoreType.DMA,
         ],
         compiler_params=pltpu.CompilerParams(
-            collective_id=0, has_side_effects=True, vmem_limit_bytes=40 * 2**20),
-    )(depth, velocity, bed, lists, listed)
+            collective_id=0, has_side_effects=True, vmem_limit_bytes=VMEM_LIMIT),
+    )(depth, velocity, bed, listed)
 
 
 def solution(mesh):

time: 40.2 us -> 36.2 us (0.900)
  local copies, waits for them, and re-layouts: 4.42 us -> 1.92 us
  Pallas kernels: 35.5 us -> 34.1 us
    unnamed x9 -> x1, local copies, waits for them, and re-layouts: 4.41 us -> 1.92 us
    pallas_call x1, Pallas kernels: 35.5 us -> 34.1 us  [shards(): pl.pallas_call(functools.partial(kernel, n), out_shape=jax.ShapeDtypeStru...]
where the time goes in v3:
time: 36.2 us; the launch traced here: 36 us
  Pallas kernels  34.1 us (94%)
  local copies, waits for them, and re-layouts  1.92 us (5%)
    pallas_call x1, Pallas kernels, shards(): pl.pallas_call(functools.partial(kernel, n), out_shape=jax.ShapeDtypeStru...  34.1 us
    unnamed x1, local copies, waits for them, and re-layouts  1.92 us

profile of v3, /device:TPU:0, one launch (start us, length us, event | category | flops | bytes accessed | tf_op | source)
XLA Modules:
  0.0 36.0 jit_solution(5939073014848498322)
XLA Ops:
  0.0 34.1 %shard_map.46 = f32[1,1,3,3,128,128]{5,4,3,2,1,0:T(8,128)} custom-call(f32[256,256]{1,0:T(8,128)} %depth_hbm.1, f32[2,256,256]{2,1,0:T(8,128)} %vel_hbm.1, f32[256,256]{1,0:T(8,128)} %bed_hbm.1, s32[3]{0:T(128)} %bitcast.1), custom_call_target="tpu_custom_call" | custom-call | tf_op jit(solution)/shard_map/pallas_call | solution.py:367
  34.1 1.9 %copy.6 = f32[1,1,3,3,128,128]{5,4,3,2,1,0:T(8,128)} copy(f32[1,1,3,3,128,128]{5,4,3,2,1,0:T(8,128)} %shard_map.46) | data formatting | bytes 1179648

commit v4 on v3

--- a/solution.py
+++ b/solution.py
@@ -16,8 +16,8 @@
 DRY_DEPTH = 0.05
 SPEED_FLOOR = 0.5
 BANDS = 18
-PART_ROWS = 64
-PART_BANDS = 10
+PART_ROWS = 32
+PART_BANDS = 6
 ROWS = 8 * PART_BANDS
 VMEM_LIMIT = 63 * 2**20
 MESH = pl.DeviceIdType.MESH
@@ -284,14 +284,14 @@
             return down, turned
 
         zeros = [jnp.zeros((8, 256), jnp.float32)] * 4
-        lax.fori_loop(0, PART_BANDS, band, (zeros, zeros), unroll=10)
+        lax.fori_loop(0, PART_BANDS, band, (zeros, zeros), unroll=6)
 
     def task(q, carry):
-        k = lax.div(q, 2)
-        first = PART_ROWS * lax.rem(q, 2)
+        k = lax.div(q, 4)
+        first = PART_ROWS * lax.rem(q, 4)
         t = jnp.where(k == 0, sent[0], jnp.where(k == 1, sent[1], jnp.where(k == 2, kept[0], kept[1])))
 
-        @pl.loop(0, PART_BANDS, unroll=5)
+        @pl.loop(0, PART_BANDS, unroll=6)
         def _(b):
             rs = pl.ds(pl.multiple_of(first + 8 * b, 8), 8)
             rd = pl.ds(pl.multiple_of(8 * b + 8, 8), 8)
@@ -300,7 +300,7 @@
 
         step(work, work.at[3])
 
-        @pl.loop(0, PART_BANDS, unroll=5)
+        @pl.loop(0, PART_BANDS, unroll=6)
         def _(b):
             rd = pl.ds(pl.multiple_of(8 * b + 8, 8), 8)
             ahead = pl.ds(pl.multiple_of(8 * b + 16, 8), 8)
@@ -311,7 +311,7 @@
 
         step(mid, work.at[3])
 
-        @pl.loop(0, 8, unroll=8)
+        @pl.loop(0, 4, unroll=4)
         def _(b):
             rd = pl.ds(pl.multiple_of(8 * b + 16, 8), 8)
             ahead = pl.ds(pl.multiple_of(8 * b + 24, 8), 8)
@@ -319,22 +319,22 @@
                 res[k, f, pl.ds(pl.multiple_of(first + 8 * b, 8), 8), :] = (
                     part[f, rd, 0:128] - from_next(face[f, rd, 0:128], face[f, ahead, 0:128]))
 
-        @pl.when(q < 4)
+        @pl.when(q < 8)
         def _():
             result_copy(q).start()
 
         return carry
 
     def result_copy(q):
-        k = lax.div(q, 2) if not isinstance(q, int) else q // 2
-        first = pl.multiple_of(PART_ROWS * (lax.rem(q, 2) if not isinstance(q, int) else q % 2), 8)
+        k = lax.div(q, 4) if not isinstance(q, int) else q // 4
+        first = pl.multiple_of(PART_ROWS * (lax.rem(q, 4) if not isinstance(q, int) else q % 4), 8)
         rows = pl.ds(first, PART_ROWS)
         return pltpu.make_async_remote_copy(
             src_ref=res.at[k, :, rows, :], dst_ref=res.at[4 + k, :, rows, :], send_sem=send_sem.at[16 + q],
             recv_sem=recv_sem.at[16 + q], device_id=at(3, 0), device_id_type=MESH)
 
-    lax.fori_loop(0, 8, task, 0)
-    for q in range(4):
+    lax.fori_loop(0, 16, task, 0)
+    for q in range(8):
         result_copy(q).wait_recv()
 
     own_rank = far_rank = jnp.int32(0)
@@ -355,7 +355,7 @@
 
     for copy in copies:
         copy.wait_send()
-    for q in range(4):
+    for q in range(8):
         result_copy(q).wait_send()
 
 
@@ -390,8 +390,8 @@
             pltpu.VMEM((3, ROWS + 16, 256), f32),
             pltpu.VMEM((3, ROWS + 16, 256), f32),
             pltpu.VMEM((6, 3, TILE, TILE), f32),
-            pltpu.SemaphoreType.DMA((20,)),
-            pltpu.SemaphoreType.DMA((20,)),
+            pltpu.SemaphoreType.DMA((24,)),
+            pltpu.SemaphoreType.DMA((24,)),
             pltpu.SemaphoreType.DMA,
         ],
         compiler_params=pltpu.CompilerParams(

time: 36.2 us -> 35.5 us (0.981)
  Pallas kernels: 34.1 us -> 33.4 us
    pallas_call x1, Pallas kernels: 34.1 us -> 33.4 us  [shards(): pl.pallas_call(functools.partial(kernel, n), out_shape=jax.ShapeDtypeStru...]
where the time goes in v4:
time: 35.5 us; the launch traced here: 35.3 us
  Pallas kernels  33.4 us (94%)
  local copies, waits for them, and re-layouts  1.92 us (5%)
    pallas_call x1, Pallas kernels, shards(): pl.pallas_call(functools.partial(kernel, n), out_shape=jax.ShapeDtypeStru...  33.4 us
    unnamed x1, local copies, waits for them, and re-layouts  1.92 us

profile of v4, /device:TPU:0, one launch (start us, length us, event | category | flops | bytes accessed | tf_op | source)
XLA Modules:
  0.0 35.3 jit_solution(1045886536069279849)
XLA Ops:
  0.0 33.4 %shard_map.46 = f32[1,1,3,3,128,128]{5,4,3,2,1,0:T(8,128)} custom-call(f32[256,256]{1,0:T(8,128)} %depth_hbm.1, f32[2,256,256]{2,1,0:T(8,128)} %vel_hbm.1, f32[256,256]{1,0:T(8,128)} %bed_hbm.1, s32[3]{0:T(128)} %bitcast.1), custom_call_target="tpu_custom_call" | custom-call | tf_op jit(solution)/shard_map/pallas_call | solution.py:367
  33.4 1.9 %copy.6 = f32[1,1,3,3,128,128]{5,4,3,2,1,0:T(8,128)} copy(f32[1,1,3,3,128,128]{5,4,3,2,1,0:T(8,128)} %shard_map.46) | data formatting | bytes 1179648

commit v5 on v4

--- a/solution.py
+++ b/solution.py
@@ -127,7 +127,6 @@
         copy.start()
         copies.append(copy)
 
-    send(colpack, colgot, 0, 1)
     send(strips.at[1], rowgot.at[0], 1, 0)
     send(strips.at[0], rowgot.at[1], 2, 0)
     send(corner.at[1], cornergot.at[0], 1, 1)
@@ -136,6 +135,7 @@
         for o in range(2):
             if k or o:
                 send(lists, listgot.at[2 * opposite[k] + o], k, o)
+    send(colpack, colgot, 0, 1)
     listgot[0] = lists[...]
 
     @pl.loop(0, 32, unroll=8)

time: 35.5 us -> 35.5 us (level)
  no operation moved by 1% of the time
where the time goes in v5:
time: 35.5 us; the launch traced here: 35.3 us
  Pallas kernels  33.4 us (94%)
  local copies, waits for them, and re-layouts  1.92 us (5%)
    pallas_call x1, Pallas kernels, shards(): pl.pallas_call(functools.partial(kernel, n), out_shape=jax.ShapeDtypeStru...  33.4 us
    unnamed x1, local copies, waits for them, and re-layouts  1.92 us

profile of v5, /device:TPU:0, one launch (start us, length us, event | category | flops | bytes accessed | tf_op | source)
XLA Modules:
  0.0 35.3 jit_solution(8698325212965753784)
XLA Ops:
  0.0 33.4 %shard_map.46 = f32[1,1,3,3,128,128]{5,4,3,2,1,0:T(8,128)} custom-call(f32[256,256]{1,0:T(8,128)} %depth_hbm.1, f32[2,256,256]{2,1,0:T(8,128)} %vel_hbm.1, f32[256,256]{1,0:T(8,128)} %bed_hbm.1, s32[3]{0:T(128)} %bitcast.1), custom_call_target="tpu_custom_call" | custom-call | tf_op jit(solution)/shard_map/pallas_call | solution.py:367
  33.4 1.9 %copy.6 = f32[1,1,3,3,128,128]{5,4,3,2,1,0:T(8,128)} copy(f32[1,1,3,3,128,128]{5,4,3,2,1,0:T(8,128)} %shard_map.46) | data formatting | bytes 1179648
